TPU v7x, 32 devices: a whole 2x2x4 slice. The times are simulated.
32 devices in a mesh: groups: 2 (over y), row: 8 (over z, x), col: 2 (over core).
Axes of the slice: x: 2, y: 2, z: 4, core: 2. Of those that a mesh axis runs over, the one named last changes fastest.
Arguments:
- coords: float32 [3, 32768], P(None, ('groups', 'row', 'col')), parts along dimension 1, may hold values from 0 to 24
- atom_types: int32 [32768], P(('groups', 'row', 'col')), parts along dimension 0, may hold values from 0 to 127
- slot_atom: int32 [32768], P(('groups', 'row', 'col')), parts along dimension 0, may hold values from 0 to 1023, as said below
- block_pairs: int32 [2, 4096], P(None, ('groups', 'row', 'col')), parts along dimension 1, may hold values from 0 to 63, as said below
- pair_count: int32 [32], P(('groups', 'row', 'col')), parts along dimension 0, may hold values from 16 to 128, as said below
- exclusion: int32 [256, 64], P(('groups', 'row', 'col')), parts along dimension 0, may hold values from 0 to 1073741823
- sigma_type: float32 [128], replicated, may hold values from 2.5 to 4
- well_type: float32 [128], replicated, may hold values from 0.1 to 0.5
- charge_type: float32 [128], replicated, may hold values from -0.8 to 0.8
Outputs:
- forces: float32 [3, 32768], P(None, ('groups', 'row', 'col')), parts along dimension 1
There are 2 independent parts, one for each index of `groups`. A program takes and returns all parts, laid end to end along the dimension named above; an argument that names none is the same for every part. Nothing has to cross between parts.
Inputs may be any that keep to these rules, and one draw needn't show every extreme that they name: `slot_atom`: the 1024 entries of each device are a permutation of 0 to 1023. `block_pairs`: entry d * 128 + s belongs to device d; row 0 is a block of its row group, below 16; row 1 is a block of its column group whose row index q // 8 differs from the device's own row index. `pair_count`: some device uses all its slots in every draw.
All inputs are finite; a program needn't handle non-finite values.
Results may differ from a plain program's by a relative error of at most 0.0003.
Values sent between devices are 32-bit elements; how exact they have to be, the bound alone decides.
A program may use at most 64 MiB of HBM per device.

v0:
```python
import functools

import jax
import jax.numpy as jnp
from jax import lax
from jax.experimental import pallas as pl
from jax.experimental.pallas import tpu as pltpu
from jax.sharding import PartitionSpec as P

COULOMB = 83.0159
CUTOFF_SQ = 144.0
CENTER = 12.0
LANES = 128
BLOCKS = 8
ROWS = 40
UNROLL = 4
MESH = pl.DeviceIdType.MESH


def lane_gather(table, lanes):
    return jnp.take_along_axis(table, lanes, axis=1, mode="promise_in_bounds")


def meet_peers(n_row, n_col):
    row, col = lax.axis_index("row"), lax.axis_index("col")
    barrier = pltpu.get_barrier_semaphore()
    for k in range(1, n_row):
        pl.semaphore_signal(
            barrier, inc=1, device_id={"row": lax.rem(row + k, n_row)}, device_id_type=MESH
        )
    for k in range(1, n_col):
        pl.semaphore_signal(
            barrier, inc=1, device_id={"col": lax.rem(col + k, n_col)}, device_id_type=MESH
        )
    pl.semaphore_wait(barrier, n_row - 1 + n_col - 1)


def exchange_kernel(
    n_row, n_col, coords_ref, types_ref, slot_ref, pairs_ref, count_ref,
    all_ref, meta_ref, send_sem, recv_sem, pass_send, pass_recv,
):
    row, col = lax.axis_index("row"), lax.axis_index("col")
    slot = slot_ref[...]
    lane, chunk = slot & (LANES - 1), slot >> 7
    mine = row * n_col + col
    kinds = types_ref[...].astype(jnp.float32)
    for comp in range(4):
        total = jnp.zeros((BLOCKS, LANES), jnp.float32)
        for r in range(BLOCKS):
            if comp < 3:
                source = coords_ref[comp : comp + 1, r * LANES : (r + 1) * LANES] - CENTER
            else:
                source = kinds[r : r + 1]
            source = jnp.broadcast_to(source, (BLOCKS, LANES))
            total = jnp.where(chunk == r, lane_gather(source, lane), total)
        all_ref[mine, comp * BLOCKS : (comp + 1) * BLOCKS, :] = total
    pairs = pairs_ref[...].astype(jnp.float32)
    count = jnp.broadcast_to(count_ref[...].astype(jnp.float32), (1, LANES))
    all_ref[mine, 32:40, :] = jnp.concatenate(
        [pairs, count, jnp.zeros((5, LANES), jnp.float32)], axis=0
    )

    meet_peers(n_row, n_col)

    def copy(slot_index, target, sems):
        return pltpu.make_async_remote_copy(
            src_ref=all_ref.at[slot_index],
            dst_ref=all_ref.at[slot_index],
            send_sem=sems[0],
            recv_sem=sems[1],
            device_id=target,
            device_id_type=MESH,
        )

    sends, passes = [], []
    for k in range(1, n_row):
        there = copy(mine, {"row": lax.rem(row + k, n_row)}, (send_sem.at[k], recv_sem.at[k]))
        there.start()
        sends.append(there)
    for k in range(n_row):
        from_row = lax.rem(row + n_row - k, n_row)
        if k:
            copy(
                from_row * n_col + col, {"row": from_row}, (send_sem.at[k], recv_sem.at[k])
            ).wait_recv()
        for j in range(1, n_col):
            on = copy(
                from_row * n_col + col,
                {"col": lax.rem(col + j, n_col)},
                (pass_send.at[k, j], pass_recv.at[k, j]),
            )
            on.start()
            passes.append(on)
    for k in range(n_row):
        from_row = lax.rem(row + n_row - k, n_row)
        for j in range(1, n_col):
            from_col = lax.rem(col + n_col - j, n_col)
            copy(
                from_row * n_col + from_col,
                {"col": from_col},
                (pass_send.at[k, j], pass_recv.at[k, j]),
            ).wait_recv()
    for there in sends + passes:
        there.wait_send()
    meta_ref[...] = all_ref[:, 32:40, :].astype(jnp.int32)


def split(value):
    high = value.astype(jnp.bfloat16).astype(jnp.float32)
    rest = value - high
    mid = rest.astype(jnp.bfloat16).astype(jnp.float32)
    return high, mid, rest - mid


def row_mask(*rows):
    index = lax.broadcasted_iota(jnp.int32, (8, LANES), 0)
    hit = index == rows[0]
    for r in rows[1:]:
        hit = hit | (index == r)
    return hit


def product_scale(weight):
    index = lax.broadcasted_iota(jnp.int32, (8, LANES), 0)
    well_scale = (4.0 * 12.0 / (CUTOFF_SQ * CUTOFF_SQ)) * weight
    charge_scale = (COULOMB / (CUTOFF_SQ * CUTOFF_SQ)) * weight
    return jnp.where(index == 6, well_scale, jnp.where(index == 7, charge_scale, 1.0))


def load_block(all_ref, table, device, block):
    x = all_ref[pl.ds(device * ROWS + block, 1), :]
    y = all_ref[pl.ds(device * ROWS + block + 8, 1), :]
    z = all_ref[pl.ds(device * ROWS + block + 16, 1), :]
    kind = all_ref[pl.ds(device * ROWS + block + 24, 1), :].astype(jnp.int32)
    params = lane_gather(table, jnp.broadcast_to(kind, (8, LANES)))
    index = lax.broadcasted_iota(jnp.int32, (8, LANES), 0)
    norm = x * x + y * y + z * z
    value = jnp.where(index == 0, x, params)
    value = jnp.where(index == 1, y, value)
    value = jnp.where(index == 2, z, value)
    value = jnp.where(index == 3, norm, value)
    return jnp.where(index == 4, 1.0, value)


def left_side(pieces):
    high, mid, low = pieces
    return jnp.concatenate([high, high, mid, mid, high, low], axis=0)


def right_side(pieces):
    index = lax.broadcasted_iota(jnp.int32, (8, LANES), 0)
    high, mid, low = pieces
    parts = []
    for piece in (high, mid, low):
        one = 1.0 if piece is high else 0.0
        for_q = jnp.where(index < 3, -2.0 * piece, 0.0)
        for_q = jnp.where(index == 3, one, for_q)
        for_q = jnp.where(index == 4, jnp.broadcast_to(piece[3:4], (8, LANES)), for_q)
        for_s = jnp.where(index == 5, one, 0.0)
        for_s = jnp.where(index == 4, jnp.broadcast_to(piece[5:6], (8, LANES)), for_s)
        for_well = jnp.where(index == 6, piece, 0.0)
        for_charge = jnp.where(index == 7, piece, 0.0)
        parts.append(jnp.concatenate([for_q, for_s, for_well, for_charge], axis=1))
    high, mid, low = parts
    return jnp.concatenate([high, mid, high, mid, low, high], axis=0)


def pair_strength(left, right, allowed=None):
    both = jnp.dot(
        left.T.astype(jnp.bfloat16), right.astype(jnp.bfloat16),
        preferred_element_type=jnp.float32,
    )
    q, s = both[:, :LANES], both[:, LANES : 2 * LANES]
    well, charge = both[:, 2 * LANES : 3 * LANES], both[:, 3 * LANES :]
    s_sq = s * s
    root = lax.rsqrt(q + s_sq)
    h = root * root
    ratio = s_sq * h
    u = ratio * ratio * ratio
    w = jnp.maximum(CUTOFF_SQ - q, 0.0)
    t = h * w + (1.0 / 3.0)
    near = (well * u) * ((u - 0.5) * t - (1.0 / 6.0))
    far = (charge * root) * (t + (11.0 / 3.0))
    g = (near + far) * w
    if allowed is not None:
        g = jnp.where(allowed, g, 0.0)
    high = g.astype(jnp.bfloat16)
    low = (g - high.astype(jnp.float32)).astype(jnp.bfloat16)
    return high, low


def both_sums(first, second, high, low):
    transposed = (((1,), (1,)), ((), ()))
    on_first = lax.dot_general(
        second, high, transposed, preferred_element_type=jnp.float32
    ) + lax.dot_general(second, low, transposed, preferred_element_type=jnp.float32)
    on_second = jnp.dot(first, high, preferred_element_type=jnp.float32) + jnp.dot(
        first, low, preferred_element_type=jnp.float32
    )
    return on_first, on_second


def force_kernel(
    n_row, n_col, place_ref, meta_ref, all_ref, excl_ref, sigma_ref, well_ref, charge_ref,
    slot_ref, force_ref, inv_ref, sums_ref, first_list, second_list,
):
    mine = place_ref[0]
    n_dev = n_row * n_col

    table = jnp.concatenate(
        [
            jnp.zeros((5, LANES), jnp.float32),
            0.5 * sigma_ref[...],
            well_ref[...],
            charge_ref[...],
        ],
        axis=0,
    )

    lane_id = lax.broadcasted_iota(jnp.int32, (16, LANES), 1)
    row_id = lax.broadcasted_iota(jnp.int32, (16, LANES), 0)
    atom_id = lax.broadcasted_iota(jnp.int32, (LANES, LANES), 0)
    slot = slot_ref[...]
    for a in range(BLOCKS):
        found = jnp.zeros((16, LANES), jnp.float32)
        for b in range(BLOCKS):
            hit = jnp.where(
                jnp.broadcast_to(slot[b : b + 1], (LANES, LANES)) == atom_id + a * LANES, 1.0, 0.0
            ).astype(jnp.bfloat16)
            names = jnp.where(row_id == 0, lane_id.astype(jnp.float32), float(b))
            found += lax.dot_general(
                names.astype(jnp.bfloat16), hit, (((1,), (1,)), ((), ())),
                preferred_element_type=jnp.float32,
            )
        whole = found[0:1] + LANES * found[1:2]
        inv_ref[a : a + 1, :] = whole.astype(jnp.int32)

    def clear(n, _):
        sums_ref[pl.ds(n * 128, 128), :] = jnp.zeros((128, LANES), jnp.float32)
        return 0

    lax.fori_loop(0, n_dev, clear, 0)

    total = lax.fori_loop(0, n_dev, lambda n, t: t + meta_ref[n, 2, 0], 0)
    start = mine * total // n_dev
    stop = (mine + 1) * total // n_dev

    def list_device(n, before):
        count = meta_ref[n, 2, 0]
        row, col = n // n_col, n % n_col

        def list_pair(s, _):
            p, q = meta_ref[n, 0, s], meta_ref[n, 1, s]
            at = before + s - start
            first_list[at] = row * (BLOCKS * n_col) + p
            second_list[at] = ((q >> 3) * n_col + col) * BLOCKS + (q & 7)
            return 0

        low = jnp.maximum(start - before, 0)
        high = jnp.minimum(count, stop - before)
        lax.fori_loop(low, high, list_pair, 0)
        return before + count

    lax.fori_loop(0, n_dev, list_device, 0)
    for extra in range(UNROLL):
        first_list[stop - start + extra] = 0
        second_list[stop - start + extra] = 0

    def add_tiles(step, _):
        found = []
        for extra in range(UNROLL):
            at = step * UNROLL + extra
            a, b = first_list[at], second_list[at]
            weight = (at < stop - start).astype(jnp.float32)
            first = split(load_block(all_ref, table, a >> 3, a & 7))
            second = split(load_block(all_ref, table, b >> 3, b & 7) * product_scale(weight))
            high, low = pair_strength(left_side(first), right_side(second))
            names = [
                jnp.concatenate(pieces[:2], axis=0).astype(jnp.bfloat16)
                for pieces in (first, second)
            ]
            found.append((a, b) + both_sums(names[0], names[1], high, low))
        for a, b, on_first, on_second in found:
            sums_ref[pl.ds(a * 16, 16), :] += on_first
            sums_ref[pl.ds(b * 16, 16), :] += on_second
        return 0

    lax.fori_loop(0, (stop - start + UNROLL - 1) // UNROLL, add_tiles, 0)

    place_i = lax.broadcasted_iota(jnp.int32, (LANES, LANES), 0)
    place_j = lax.broadcasted_iota(jnp.int32, (LANES, LANES), 1)
    gap = place_j - place_i
    bit = (place_i & 1) * 15 + jnp.clip(gap - 1, 0, 14)
    excl = excl_ref[...]
    half_i = lax.broadcasted_iota(jnp.int32, (LANES, 64), 0) >> 1
    half_k = lax.broadcasted_iota(jnp.int32, (LANES, 64), 1)
    pick = half_i == half_k
    for b in range(BLOCKS):
        words = jnp.broadcast_to(excl[b : b + 1], (LANES, 64))
        word = jnp.sum(jnp.where(pick, words >> 15, 0).astype(jnp.float32), axis=1, keepdims=True)
        word_low = jnp.sum(
            jnp.where(pick, words & 32767, 0).astype(jnp.float32), axis=1, keepdims=True
        )
        odd = lax.broadcasted_iota(jnp.int32, (LANES, 1), 0) & 1
        mine15 = jnp.where(odd == 1, word, word_low).astype(jnp.int32)
        bits = (jnp.broadcast_to(mine15, (LANES, LANES)) >> jnp.clip(gap - 1, 0, 14)) & 1
        allowed = (gap >= 1) & ((gap > 15) | (bits == 0))
        value = load_block(all_ref, table, mine, b)
        pieces = split(value)
        right = right_side(split(value * product_scale(1.0)))
        high, low = pair_strength(left_side(pieces), right, allowed)
        names = jnp.concatenate(pieces[:2], axis=0).astype(jnp.bfloat16)
        on_first, on_second = both_sums(names, names, high, low)
        at = pl.ds((mine * BLOCKS + b) * 16, 16)
        sums_ref[at, :] += on_first + on_second

    def finish(n, _):
        def rows(r):
            return sums_ref[pl.ds(n * 128 + r, BLOCKS, stride=16), :]

        g_sum = rows(4)
        for comp in range(3):
            x = all_ref[pl.ds(n * ROWS + comp * BLOCKS, BLOCKS), :]
            force_ref[n, comp * BLOCKS : (comp + 1) * BLOCKS, :] = (
                x * g_sum - rows(comp) - rows(comp + 8)
            )
        return 0

    lax.fori_loop(0, n_dev, finish, 0)


def return_kernel(
    n_row, n_col, force_ref, inv_ref, out_ref,
    core_buf, send_buf, row_buf, core_send, core_recv, row_send, row_recv,
):
    row, col = lax.axis_index("row"), lax.axis_index("col")
    meet_peers(n_row, n_col)
    sends = []
    order = list(range(1, n_row)) + [0]
    for k in order:
        to_row = lax.rem(row + k, n_row)
        for j in range(1, n_col):
            to_col = lax.rem(col + j, n_col)
            there = pltpu.make_async_remote_copy(
                src_ref=force_ref.at[to_row * n_col + to_col],
                dst_ref=core_buf.at[k, j],
                send_sem=core_send.at[k, j],
                recv_sem=core_recv.at[k, j],
                device_id={"col": to_col},
                device_id_type=MESH,
            )
            there.start()
            sends.append(there)
    arrive = []
    own = None
    at = 0
    for k in order:
        to_row = lax.rem(row + k, n_row)
        part = force_ref[to_row * n_col + col]
        for j in range(1, n_col):
            sends[at].wait_recv()
            at += 1
            part = part + core_buf[k, j]
        if k == 0:
            own = part
        else:
            send_buf[k] = part
            there = pltpu.make_async_remote_copy(
                src_ref=send_buf.at[k],
                dst_ref=row_buf.at[k],
                send_sem=row_send.at[k],
                recv_sem=row_recv.at[k],
                device_id={"row": to_row},
                device_id_type=MESH,
            )
            there.start()
            arrive.append(there)
    for k in range(1, n_row):
        arrive[k - 1].wait_recv()
        own = own + row_buf[k]
    for there in sends + arrive:
        there.wait_send()
    inverse = inv_ref[...]
    lane, chunk = inverse & (LANES - 1), inverse >> 7
    for comp in range(3):
        total = jnp.zeros((BLOCKS, LANES), jnp.float32)
        for r in range(BLOCKS):
            at = comp * BLOCKS + r
            source = jnp.broadcast_to(own[at : at + 1], (BLOCKS, LANES))
            total = jnp.where(chunk == r, lane_gather(source, lane), total)
        for r in range(BLOCKS):
            out_ref[comp : comp + 1, r * LANES : (r + 1) * LANES] = total[r : r + 1]


def body(n_row, n_col, coords, atom_types, slot_atom, block_pairs, pair_count, exclusion,
         sigma_type, well_type, charge_type):
    n_dev = n_row * n_col
    slots = slot_atom.reshape(BLOCKS, LANES)
    vmem = pl.BlockSpec(memory_space=pltpu.VMEM)
    smem = pl.BlockSpec(memory_space=pltpu.SMEM)
    dma = pltpu.SemaphoreType.DMA
    gathered, meta = pl.pallas_call(
        functools.partial(exchange_kernel, n_row, n_col),
        out_shape=(
            jax.ShapeDtypeStruct((n_dev, ROWS, LANES), jnp.float32),
            jax.ShapeDtypeStruct((n_dev, 8, LANES), jnp.int32),
        ),
        in_specs=[vmem] * 5,
        out_specs=(vmem, vmem),
        scratch_shapes=[
            dma((n_row,)), dma((n_row,)), dma((n_row, n_col)), dma((n_row, n_col)),
        ],
        compiler_params=pltpu.CompilerParams(
            collective_id=0, has_side_effects=True, vmem_limit_bytes=32 << 20
        ),
        name="exchange",
    )(coords, atom_types.reshape(BLOCKS, LANES), slots, block_pairs, pair_count.reshape(1, 1))
    place = (lax.axis_index("row") * n_col + lax.axis_index("col")).reshape(1)
    most = block_pairs.shape[1]
    force, inverse = pl.pallas_call(
        functools.partial(force_kernel, n_row, n_col),
        out_shape=(
            jax.ShapeDtypeStruct((n_dev, 24, LANES), jnp.float32),
            jax.ShapeDtypeStruct((BLOCKS, LANES), jnp.int32),
        ),
        in_specs=[smem, smem] + [vmem] * 6,
        out_specs=(vmem, vmem),
        scratch_shapes=[
            pltpu.VMEM((n_dev * 128, LANES), jnp.float32),
            pltpu.SMEM((most + 1 + UNROLL,), jnp.int32),
            pltpu.SMEM((most + 1 + UNROLL,), jnp.int32),
        ],
        compiler_params=pltpu.CompilerParams(vmem_limit_bytes=48 << 20),
        name="pair_forces",
    )(
        place, meta, gathered.reshape(n_dev * ROWS, LANES), exclusion,
        sigma_type.reshape(1, LANES), well_type.reshape(1, LANES),
        charge_type.reshape(1, LANES), slots,
    )
    return pl.pallas_call(
        functools.partial(return_kernel, n_row, n_col),
        out_shape=jax.ShapeDtypeStruct(coords.shape, jnp.float32),
        in_specs=[vmem, vmem],
        out_specs=vmem,
        scratch_shapes=[
            pltpu.VMEM((n_row, n_col, 24, LANES), jnp.float32),
            pltpu.VMEM((n_row, 24, LANES), jnp.float32),
            pltpu.VMEM((n_row, 24, LANES), jnp.float32),
            dma((n_row, n_col)), dma((n_row, n_col)), dma((n_row,)), dma((n_row,)),
        ],
        compiler_params=pltpu.CompilerParams(
            collective_id=1, has_side_effects=True, vmem_limit_bytes=32 << 20
        ),
        name="return_forces",
    )(force, inverse)


def solution(mesh):
    every = ("groups", "row", "col")
    return jax.shard_map(
        functools.partial(body, mesh.shape["row"], mesh.shape["col"]),
        mesh=mesh,
        in_specs=(
            P(None, every), P(every), P(every), P(None, every), P(every), P(every, None),
            P(), P(), P(),
        ),
        out_specs=P(None, every),
        check_vma=False,
    )
```

profile of v0, /device:TPU:0, one launch (start us, length us, event | category | flops | bytes accessed | tf_op | source)
XLA Modules:
  0.0 41.6 jit_solution(10461825855614739246)
XLA Ops:
  0.0 0.0 copy-start.1
  0.7 0.0 copy-start.3
  0.7 0.0 copy-start
  0.7 0.0 copy-start.4
  0.7 0.0 copy-done.1
  0.7 0.6 %copy-done.3 = s32[1024]{0:T(1024)S(1)} copy-done((s32[1024]{0:T(1024)S(1)}, s32[1024]{0:T(1024)}, u32[]{:S(2)}) %copy-start.3) | copy-done | bytes 4120
  1.4 0.0 copy-done
  1.4 0.0 copy-done.4
  1.4 11.2 %exchange.1 = (f32[16,40,128]{2,1,0:T(8,128)S(1)}, s32[16,8,128]{2,1,0:T(8,128)S(1)}) custom-call(f32[3,1024]{1,0:T(4,128)S(1)} %copy-done.1, s32[8,128]{1,0:T(8,128)S(1)} %bitcast.12, s32[8,128]{1,0:T(8,128)S(1)} %bitcast.10, s32[2,128]{1,0:T(2,128)S(1)} %copy-done.4, s32[1,1]{1,0:T(1,128)} %bitcast.8.count_ref), custom_call_target="tpu_custom_call" | custom-call | tf_op jit(solution)/shard_map/exchange/pallas_call | solution.py:402
  12.6 0.0 copy-start.2
  12.6 0.0 copy-start.5
  12.6 0.0 copy-start.6
  12.6 0.0 copy-start.7
  12.6 0.6 %copy-done.2 = s32[8,64]{1,0:T(8,128)S(1)} copy-done((s32[8,64]{1,0:T(8,128)S(1)}, s32[8,64]{1,0:T(8,128)}, u32[]{:S(2)}) %copy-start.2) | copy-done | bytes 2072
  13.3 0.0 copy-done.5
  13.3 0.0 copy-done.6
  13.3 0.0 copy-done.7
  13.3 18.8 %pair_forces.1 = (f32[16,24,128]{2,1,0:T(8,128)S(1)}, s32[8,128]{1,0:T(8,128)S(1)}) custom-call(s32[1]{0:T(128)} %bitcast.place_ref, s32[16,8,128]{2,1,0:T(8,128)S(1)} %get-tuple-element.9.meta_ref, f32[640,128]{1,0:T(8,128)S(1)} %bitcast.9, s32[8,64]{1,0:T(8,128)S(1)} %copy-done.2, f32[1,128]{1,0:T(1,128)S(1)} %bitcast.13, f32[1,128]{1,0:T(1,128)S(1)} %bitcast.14, ...), custom_call_target="tpu_custom_call" | custom-call | tf_op jit(solution)/shard_map/pair_forces/pallas_call | solution.py:420
  32.1 8.9 %return_forces.1 = f32[3,1024]{1,0:T(4,128)S(1)} custom-call(f32[16,24,128]{2,1,0:T(8,128)S(1)} %get-tuple-element.11.force_ref, s32[8,128]{1,0:T(8,128)S(1)} %get-tuple-element.12.inv_ref), custom_call_target="tpu_custom_call" | custom-call | tf_op jit(solution)/shard_map/return_forces/pallas_call | solution.py:440
  40.9 0.6 %copy.12 = f32[3,1024]{1,0:T(4,128)} copy(f32[3,1024]{1,0:T(4,128)S(1)} %return_forces.1) | data formatting | bytes 24576
Async XLA Ops:
  0.0 0.7 %copy-start.1 = (f32[3,1024]{1,0:T(4,128)S(1)}, f32[3,1024]{1,0:T(4,128)}, u32[]{:S(2)}) copy-start(f32[3,1024]{1,0:T(4,128)} %coords_ref.1) | copy-start | bytes 36868
  0.7 0.7 %copy-start.3 = (s32[1024]{0:T(1024)S(1)}, s32[1024]{0:T(1024)}, u32[]{:S(2)}) copy-start(s32[1024]{0:T(1024)} %param.10) | copy-start | bytes 12292
  0.7 0.7 %copy-start = (s32[1024]{0:T(1024)S(1)}, s32[1024]{0:T(1024)}, u32[]{:S(2)}) copy-start(s32[1024]{0:T(1024)} %param.11) | copy-start | bytes 12292
  0.7 0.7 %copy-start.4 = (s32[2,128]{1,0:T(2,128)S(1)}, s32[2,128]{1,0:T(2,128)}, u32[]{:S(2)}) copy-start(s32[2,128]{1,0:T(2,128)} %pairs_ref.1) | copy-start | bytes 3076
  12.6 0.7 %copy-start.2 = (s32[8,64]{1,0:T(8,128)S(1)}, s32[8,64]{1,0:T(8,128)}, u32[]{:S(2)}) copy-start(s32[8,64]{1,0:T(8,128)} %excl_ref.1) | copy-start | bytes 6148
  12.6 0.7 %copy-start.5 = (f32[128]{0:T(128)S(1)}, f32[128]{0:T(128)}, u32[]{:S(2)}) copy-start(f32[128]{0:T(128)} %param.15) | copy-start | bytes 1540
  12.6 0.7 %copy-start.6 = (f32[128]{0:T(128)S(1)}, f32[128]{0:T(128)}, u32[]{:S(2)}) copy-start(f32[128]{0:T(128)} %param.16) | copy-start | bytes 1540
  12.6 0.7 %copy-start.7 = (f32[128]{0:T(128)S(1)}, f32[128]{0:T(128)}, u32[]{:S(2)}) copy-start(f32[128]{0:T(128)} %param.17) | copy-start | bytes 1540
where the time goes:
time: 42 us; the launch traced here: 41.6 us
  Pallas kernels  38.8 us (92%)
  local copies, waits for them, and re-layouts  1.97 us (5%)
  between operations  0.74 us (2%)
    pallas_call x1, Pallas kernels, body(): pl.pallas_call(functools.partial(force_kernel, n_row, n_col), out_shape=(...  18.8 us
    pallas_call x1, Pallas kernels, body(): pl.pallas_call(functools.partial(exchange_kernel, n_row, n_col), out_shap...  11.2 us
    pallas_call x1, Pallas kernels, body(): pl.pallas_call(functools.partial(return_kernel, n_row, n_col), out_shape=...  8.87 us
    unnamed x17, local copies, waits for them, and re-layouts  1.97 us

commit v1 on v0

--- a/solution.py
+++ b/solution.py
@@ -13,7 +13,7 @@
 LANES = 128
 BLOCKS = 8
 ROWS = 40
-UNROLL = 4
+UNROLL = 8
 MESH = pl.DeviceIdType.MESH
 
 
@@ -21,7 +21,7 @@
     return jnp.take_along_axis(table, lanes, axis=1, mode="promise_in_bounds")
 
 
-def meet_peers(n_row, n_col):
+def greet_peers(n_row, n_col):
     row, col = lax.axis_index("row"), lax.axis_index("col")
     barrier = pltpu.get_barrier_semaphore()
     for k in range(1, n_row):
@@ -32,15 +32,17 @@
         pl.semaphore_signal(
             barrier, inc=1, device_id={"col": lax.rem(col + k, n_col)}, device_id_type=MESH
         )
-    pl.semaphore_wait(barrier, n_row - 1 + n_col - 1)
+    return barrier
 
 
 def exchange_kernel(
-    n_row, n_col, coords_ref, types_ref, slot_ref, pairs_ref, count_ref,
-    all_ref, meta_ref, send_sem, recv_sem, pass_send, pass_recv,
+    n_row, n_col, coords_ref, types_ref, slot_ref, pairs_ref, count_ref, excl_ref,
+    sigma_ref, well_ref, charge_ref, all_ref, meta_ref, own_ref, inv_ref, send_sem, recv_sem, pass_send, pass_recv,
 ):
     row, col = lax.axis_index("row"), lax.axis_index("col")
+    barrier = greet_peers(n_row, n_col)
     slot = slot_ref[...]
+    own = []
     lane, chunk = slot & (LANES - 1), slot >> 7
     mine = row * n_col + col
     kinds = types_ref[...].astype(jnp.float32)
@@ -54,13 +56,14 @@
             source = jnp.broadcast_to(source, (BLOCKS, LANES))
             total = jnp.where(chunk == r, lane_gather(source, lane), total)
         all_ref[mine, comp * BLOCKS : (comp + 1) * BLOCKS, :] = total
+        own.append(total)
     pairs = pairs_ref[...].astype(jnp.float32)
     count = jnp.broadcast_to(count_ref[...].astype(jnp.float32), (1, LANES))
     all_ref[mine, 32:40, :] = jnp.concatenate(
         [pairs, count, jnp.zeros((5, LANES), jnp.float32)], axis=0
     )
 
-    meet_peers(n_row, n_col)
+    pl.semaphore_wait(barrier, n_row - 1 + n_col - 1)
 
     def copy(slot_index, target, sems):
         return pltpu.make_async_remote_copy(
@@ -79,6 +82,8 @@
         sends.append(there)
     for k in range(n_row):
         from_row = lax.rem(row + n_row - k, n_row)
+        if k == 1:
+            own_pairs(own, excl_ref, type_rows(sigma_ref, well_ref, charge_ref), own_ref)
         if k:
             copy(
                 from_row * n_col + col, {"row": from_row}, (send_sem.at[k], recv_sem.at[k])
@@ -91,6 +96,7 @@
             )
             on.start()
             passes.append(on)
+    invert(slot, inv_ref)
     for k in range(n_row):
         from_row = lax.rem(row + n_row - k, n_row)
         for j in range(1, n_col):
@@ -127,11 +133,27 @@
     return jnp.where(index == 6, well_scale, jnp.where(index == 7, charge_scale, 1.0))
 
 
+def type_rows(sigma_ref, well_ref, charge_ref):
+    return jnp.concatenate(
+        [
+            jnp.zeros((5, LANES), jnp.float32),
+            0.5 * sigma_ref[...],
+            well_ref[...],
+            charge_ref[...],
+        ],
+        axis=0,
+    )
+
+
 def load_block(all_ref, table, device, block):
-    x = all_ref[pl.ds(device * ROWS + block, 1), :]
-    y = all_ref[pl.ds(device * ROWS + block + 8, 1), :]
-    z = all_ref[pl.ds(device * ROWS + block + 16, 1), :]
-    kind = all_ref[pl.ds(device * ROWS + block + 24, 1), :].astype(jnp.int32)
+    return block_rows(
+        [all_ref[pl.ds(device * ROWS + block + 8 * comp, 1), :] for comp in range(4)], table
+    )
+
+
+def block_rows(parts, table):
+    x, y, z, kind = parts
+    kind = kind.astype(jnp.int32)
     params = lane_gather(table, jnp.broadcast_to(kind, (8, LANES)))
     index = lax.broadcasted_iota(jnp.int32, (8, LANES), 0)
     norm = x * x + y * y + z * z
@@ -190,37 +212,22 @@
 
 
 def both_sums(first, second, high, low):
-    transposed = (((1,), (1,)), ((), ()))
+    high_low = jnp.concatenate([high, low], axis=1)
     on_first = lax.dot_general(
-        second, high, transposed, preferred_element_type=jnp.float32
-    ) + lax.dot_general(second, low, transposed, preferred_element_type=jnp.float32)
-    on_second = jnp.dot(first, high, preferred_element_type=jnp.float32) + jnp.dot(
-        first, low, preferred_element_type=jnp.float32
+        jnp.concatenate([second, second], axis=1), high_low, (((1,), (1,)), ((), ())),
+        preferred_element_type=jnp.float32,
+    )
+    on_second = jnp.dot(
+        jnp.concatenate([first, first], axis=1), jnp.concatenate([high, low], axis=0),
+        preferred_element_type=jnp.float32,
     )
     return on_first, on_second
 
 
-def force_kernel(
-    n_row, n_col, place_ref, meta_ref, all_ref, excl_ref, sigma_ref, well_ref, charge_ref,
-    slot_ref, force_ref, inv_ref, sums_ref, first_list, second_list,
-):
-    mine = place_ref[0]
-    n_dev = n_row * n_col
-
-    table = jnp.concatenate(
-        [
-            jnp.zeros((5, LANES), jnp.float32),
-            0.5 * sigma_ref[...],
-            well_ref[...],
-            charge_ref[...],
-        ],
-        axis=0,
-    )
-
+def invert(slot, inv_ref):
     lane_id = lax.broadcasted_iota(jnp.int32, (16, LANES), 1)
     row_id = lax.broadcasted_iota(jnp.int32, (16, LANES), 0)
     atom_id = lax.broadcasted_iota(jnp.int32, (LANES, LANES), 0)
-    slot = slot_ref[...]
     for a in range(BLOCKS):
         found = jnp.zeros((16, LANES), jnp.float32)
         for b in range(BLOCKS):
@@ -235,11 +242,49 @@
         whole = found[0:1] + LANES * found[1:2]
         inv_ref[a : a + 1, :] = whole.astype(jnp.int32)
 
+
+def own_pairs(own, excl_ref, table, own_ref):
+    place_i = lax.broadcasted_iota(jnp.int32, (LANES, LANES), 0)
+    place_j = lax.broadcasted_iota(jnp.int32, (LANES, LANES), 1)
+    gap = place_j - place_i
+    excl = excl_ref[...]
+    half_i = lax.broadcasted_iota(jnp.int32, (LANES, 64), 0) >> 1
+    half_k = lax.broadcasted_iota(jnp.int32, (LANES, 64), 1)
+    pick = half_i == half_k
+    for b in range(BLOCKS):
+        words = jnp.broadcast_to(excl[b : b + 1], (LANES, 64))
+        word = jnp.sum(jnp.where(pick, words >> 15, 0).astype(jnp.float32), axis=1, keepdims=True)
+        word_low = jnp.sum(
+            jnp.where(pick, words & 32767, 0).astype(jnp.float32), axis=1, keepdims=True
+        )
+        odd = lax.broadcasted_iota(jnp.int32, (LANES, 1), 0) & 1
+        mine15 = jnp.where(odd == 1, word, word_low).astype(jnp.int32)
+        bits = (jnp.broadcast_to(mine15, (LANES, LANES)) >> jnp.clip(gap - 1, 0, 14)) & 1
+        allowed = (gap >= 1) & ((gap > 15) | (bits == 0))
+        value = block_rows([part[b : b + 1] for part in own], table)
+        pieces = split(value)
+        right = right_side(split(value * product_scale(1.0)))
+        high, low = pair_strength(left_side(pieces), right, allowed)
+        names = jnp.concatenate(pieces[:2], axis=0).astype(jnp.bfloat16)
+        on_first, on_second = both_sums(names, names, high, low)
+        own_ref[b * 16 : (b + 1) * 16, :] = on_first + on_second
+
+
+def force_kernel(
+    n_row, n_col, place_ref, meta_ref, all_ref, sigma_ref, well_ref, charge_ref,
+    own_ref, force_ref, sums_ref, first_list, second_list,
+):
+    mine = place_ref[0]
+    n_dev = n_row * n_col
+
+    table = type_rows(sigma_ref, well_ref, charge_ref)
+
     def clear(n, _):
         sums_ref[pl.ds(n * 128, 128), :] = jnp.zeros((128, LANES), jnp.float32)
         return 0
 
     lax.fori_loop(0, n_dev, clear, 0)
+    sums_ref[pl.ds(mine * 128, 128), :] = own_ref[...]
 
     total = lax.fori_loop(0, n_dev, lambda n, t: t + meta_ref[n, 2, 0], 0)
     start = mine * total // n_dev
@@ -287,33 +332,6 @@
 
     lax.fori_loop(0, (stop - start + UNROLL - 1) // UNROLL, add_tiles, 0)
 
-    place_i = lax.broadcasted_iota(jnp.int32, (LANES, LANES), 0)
-    place_j = lax.broadcasted_iota(jnp.int32, (LANES, LANES), 1)
-    gap = place_j - place_i
-    bit = (place_i & 1) * 15 + jnp.clip(gap - 1, 0, 14)
-    excl = excl_ref[...]
-    half_i = lax.broadcasted_iota(jnp.int32, (LANES, 64), 0) >> 1
-    half_k = lax.broadcasted_iota(jnp.int32, (LANES, 64), 1)
-    pick = half_i == half_k
-    for b in range(BLOCKS):
-        words = jnp.broadcast_to(excl[b : b + 1], (LANES, 64))
-        word = jnp.sum(jnp.where(pick, words >> 15, 0).astype(jnp.float32), axis=1, keepdims=True)
-        word_low = jnp.sum(
-            jnp.where(pick, words & 32767, 0).astype(jnp.float32), axis=1, keepdims=True
-        )
-        odd = lax.broadcasted_iota(jnp.int32, (LANES, 1), 0) & 1
-        mine15 = jnp.where(odd == 1, word, word_low).astype(jnp.int32)
-        bits = (jnp.broadcast_to(mine15, (LANES, LANES)) >> jnp.clip(gap - 1, 0, 14)) & 1
-        allowed = (gap >= 1) & ((gap > 15) | (bits == 0))
-        value = load_block(all_ref, table, mine, b)
-        pieces = split(value)
-        right = right_side(split(value * product_scale(1.0)))
-        high, low = pair_strength(left_side(pieces), right, allowed)
-        names = jnp.concatenate(pieces[:2], axis=0).astype(jnp.bfloat16)
-        on_first, on_second = both_sums(names, names, high, low)
-        at = pl.ds((mine * BLOCKS + b) * 16, 16)
-        sums_ref[at, :] += on_first + on_second
-
     def finish(n, _):
         def rows(r):
             return sums_ref[pl.ds(n * 128 + r, BLOCKS, stride=16), :]
@@ -334,7 +352,8 @@
     core_buf, send_buf, row_buf, core_send, core_recv, row_send, row_recv,
 ):
     row, col = lax.axis_index("row"), lax.axis_index("col")
-    meet_peers(n_row, n_col)
+    barrier = greet_peers(n_row, n_col)
+    pl.semaphore_wait(barrier, n_row - 1 + n_col - 1)
     sends = []
     order = list(range(1, n_row)) + [0]
     for k in order:
@@ -399,14 +418,17 @@
     vmem = pl.BlockSpec(memory_space=pltpu.VMEM)
     smem = pl.BlockSpec(memory_space=pltpu.SMEM)
     dma = pltpu.SemaphoreType.DMA
-    gathered, meta = pl.pallas_call(
+    tables = [t.reshape(1, LANES) for t in (sigma_type, well_type, charge_type)]
+    gathered, meta, own, inverse = pl.pallas_call(
         functools.partial(exchange_kernel, n_row, n_col),
         out_shape=(
             jax.ShapeDtypeStruct((n_dev, ROWS, LANES), jnp.float32),
             jax.ShapeDtypeStruct((n_dev, 8, LANES), jnp.int32),
+            jax.ShapeDtypeStruct((BLOCKS * 16, LANES), jnp.float32),
+            jax.ShapeDtypeStruct((BLOCKS, LANES), jnp.int32),
         ),
-        in_specs=[vmem] * 5,
-        out_specs=(vmem, vmem),
+        in_specs=[vmem] * 9,
+        out_specs=(vmem,) * 4,
         scratch_shapes=[
             dma((n_row,)), dma((n_row,)), dma((n_row, n_col)), dma((n_row, n_col)),
         ],
@@ -414,17 +436,15 @@
             collective_id=0, has_side_effects=True, vmem_limit_bytes=32 << 20
         ),
         name="exchange",
-    )(coords, atom_types.reshape(BLOCKS, LANES), slots, block_pairs, pair_count.reshape(1, 1))
+    )(coords, atom_types.reshape(BLOCKS, LANES), slots, block_pairs, pair_count.reshape(1, 1),
+      exclusion, *tables)
     place = (lax.axis_index("row") * n_col + lax.axis_index("col")).reshape(1)
     most = block_pairs.shape[1]
-    force, inverse = pl.pallas_call(
+    force = pl.pallas_call(
         functools.partial(force_kernel, n_row, n_col),
-        out_shape=(
-            jax.ShapeDtypeStruct((n_dev, 24, LANES), jnp.float32),
-            jax.ShapeDtypeStruct((BLOCKS, LANES), jnp.int32),
-        ),
-        in_specs=[smem, smem] + [vmem] * 6,
-        out_specs=(vmem, vmem),
+        out_shape=jax.ShapeDtypeStruct((n_dev, 24, LANES), jnp.float32),
+        in_specs=[smem, smem] + [vmem] * 5,
+        out_specs=vmem,
         scratch_shapes=[
             pltpu.VMEM((n_dev * 128, LANES), jnp.float32),
             pltpu.SMEM((most + 1 + UNROLL,), jnp.int32),
@@ -433,9 +453,7 @@
         compiler_params=pltpu.CompilerParams(vmem_limit_bytes=48 << 20),
         name="pair_forces",
     )(
-        place, meta, gathered.reshape(n_dev * ROWS, LANES), exclusion,
-        sigma_type.reshape(1, LANES), well_type.reshape(1, LANES),
-        charge_type.reshape(1, LANES), slots,
+        place, meta, gathered.reshape(n_dev * ROWS, LANES), *tables, own,
     )
     return pl.pallas_call(
         functools.partial(return_kernel, n_row, n_col),

time: 42 us -> 37.6 us (0.90)
  Pallas kernels: 38.8 us -> 34.6 us
    pallas_call x1, Pallas kernels: 18.8 us -> 14.4 us  [body(): pl.pallas_call(functools.partial(force_kernel, n_row, n_col), out_shape=j...]
where the time goes in v1:
time: 37.6 us; the launch traced here: 37.3 us
  Pallas kernels  34.6 us (92%)
  local copies, waits for them, and re-layouts  1.94 us (5%)
  between operations  0.78 us (2%)
    pallas_call x1, Pallas kernels, body(): pl.pallas_call(functools.partial(force_kernel, n_row, n_col), out_shape=j...  14.4 us
    pallas_call x1, Pallas kernels, body(): pl.pallas_call(functools.partial(exchange_kernel, n_row, n_col), out_shap...  11.3 us
    pallas_call x1, Pallas kernels, body(): pl.pallas_call(functools.partial(return_kernel, n_row, n_col), out_shape=...  8.89 us
    unnamed x17, local copies, waits for them, and re-layouts  1.94 us

profile of v1, /device:TPU:0, one launch (start us, length us, event | category | flops | bytes accessed | tf_op | source)
XLA Modules:
  0.0 37.3 jit_solution(1315955198501825063)
XLA Ops:
  0.0 0.0 copy-start
  0.0 0.0 copy-start.6
  0.0 0.0 copy-start.3
  0.7 0.0 copy-start.2
  0.7 0.0 copy-start.1
  0.7 0.0 copy-start.4
  0.7 0.0 copy-start.5
  0.7 0.0 copy-done
  0.7 0.0 copy-done.6
  0.8 0.0 copy-done.3
  0.8 0.6 %copy-done.2 = s32[1024]{0:T(1024)S(1)} copy-done((s32[1024]{0:T(1024)S(1)}, s32[1024]{0:T(1024)}, u32[]{:S(2)}) %copy-start.2) | copy-done | bytes 4120
  1.4 0.0 copy-done.1
  1.4 0.0 copy-done.4
  1.4 0.0 copy-done.5
  1.4 0.0 copy-start.7
  1.4 0.7 %copy-done.7 = s32[2,128]{1,0:T(2,128)S(1)} copy-done((s32[2,128]{1,0:T(2,128)S(1)}, s32[2,128]{1,0:T(2,128)}, u32[]{:S(2)}) %copy-start.7) | copy-done | bytes 1048
  2.1 11.3 %exchange.1 = (f32[16,40,128]{2,1,0:T(8,128)S(1)}, s32[16,8,128]{2,1,0:T(8,128)S(1)}, f32[128,128]{1,0:T(8,128)S(1)}, s32[8,128]{1,0:T(8,128)S(1)}) custom-call(f32[3,1024]{1,0:T(4,128)S(1)} %copy-done, s32[8,128]{1,0:T(8,128)S(1)} %bitcast.10, s32[8,128]{1,0:T(8,128)S(1)} %bitcast.11, s32[2,128]{1,0:T(2,128)S(1)} %copy-done.7, s32[1,1]{1,0:T(1,128)} %bitcast.8.count_ref, ...), custom_call_target="tpu_custom_call" | custom-call | tf_op jit(solution)/shard_map/exchange/pallas_call | solution.py:422
  13.4 14.4 %pair_forces.1.force_ref = f32[16,24,128]{2,1,0:T(8,128)S(1)} custom-call(s32[1]{0:T(128)} %bitcast.place_ref, s32[16,8,128]{2,1,0:T(8,128)S(1)} %get-tuple-element.9.meta_ref, f32[640,128]{1,0:T(8,128)S(1)} %bitcast.9, f32[1,128]{1,0:T(1,128)S(1)} %bitcast.13, f32[1,128]{1,0:T(1,128)S(1)} %bitcast.15, f32[1,128]{1,0:T(1,128)S(1)} %bitcast.17, ...), custom_call_target="tpu_custom_call" | custom-call | tf_op jit(solution)/shard_map/pair_forces/pallas_call | solution.py:443
  27.8 8.9 %return_forces.1 = f32[3,1024]{1,0:T(4,128)S(1)} custom-call(f32[16,24,128]{2,1,0:T(8,128)S(1)} %pair_forces.1.force_ref, s32[8,128]{1,0:T(8,128)S(1)} %get-tuple-element.12.inv_ref), custom_call_target="tpu_custom_call" | custom-call | tf_op jit(solution)/shard_map/return_forces/pallas_call | solution.py:458
  36.7 0.6 %copy.12 = f32[3,1024]{1,0:T(4,128)} copy(f32[3,1024]{1,0:T(4,128)S(1)} %return_forces.1) | data formatting | bytes 24576
Async XLA Ops:
  0.0 0.7 %copy-start = (f32[3,1024]{1,0:T(4,128)S(1)}, f32[3,1024]{1,0:T(4,128)}, u32[]{:S(2)}) copy-start(f32[3,1024]{1,0:T(4,128)} %coords_ref.1) | copy-start | bytes 36868
  0.0 0.7 %copy-start.6 = (f32[128]{0:T(128)S(1)}, f32[128]{0:T(128)}, u32[]{:S(2)}) copy-start(f32[128]{0:T(128)} %param.17) | copy-start | bytes 1540
  0.0 0.8 %copy-start.3 = (s32[8,64]{1,0:T(8,128)S(1)}, s32[8,64]{1,0:T(8,128)}, u32[]{:S(2)}) copy-start(s32[8,64]{1,0:T(8,128)} %excl_ref.1) | copy-start | bytes 6148
  0.7 0.7 %copy-start.2 = (s32[1024]{0:T(1024)S(1)}, s32[1024]{0:T(1024)}, u32[]{:S(2)}) copy-start(s32[1024]{0:T(1024)} %param.11) | copy-start | bytes 12292
  0.7 0.7 %copy-start.1 = (s32[1024]{0:T(1024)S(1)}, s32[1024]{0:T(1024)}, u32[]{:S(2)}) copy-start(s32[1024]{0:T(1024)} %param.10) | copy-start | bytes 12292
  0.7 0.7 %copy-start.4 = (f32[128]{0:T(128)S(1)}, f32[128]{0:T(128)}, u32[]{:S(2)}) copy-start(f32[128]{0:T(128)} %param.15) | copy-start | bytes 1540
  0.7 0.7 %copy-start.5 = (f32[128]{0:T(128)S(1)}, f32[128]{0:T(128)}, u32[]{:S(2)}) copy-start(f32[128]{0:T(128)} %param.16) | copy-start | bytes 1540
  1.4 0.7 %copy-start.7 = (s32[2,128]{1,0:T(2,128)S(1)}, s32[2,128]{1,0:T(2,128)}, u32[]{:S(2)}) copy-start(s32[2,128]{1,0:T(2,128)} %pairs_ref.1) | copy-start | bytes 3076

commit v2 on v1

--- a/solution.py
+++ b/solution.py
@@ -36,11 +36,21 @@
 
 
 def exchange_kernel(
-    n_row, n_col, coords_ref, types_ref, slot_ref, pairs_ref, count_ref, excl_ref,
-    sigma_ref, well_ref, charge_ref, all_ref, meta_ref, own_ref, inv_ref, send_sem, recv_sem, pass_send, pass_recv,
+    n_row, n_col, count_ref, *refs,
 ):
+    inputs, (all_ref, meta_ref, own_ref, inv_ref), local = refs[:8], refs[8:12], refs[12:20]
+    load_sem, send_sem, recv_sem, pass_send, pass_recv = refs[20:]
+    loads = [
+        pltpu.make_async_copy(source, target, load_sem.at[k])
+        for k, (source, target) in enumerate(zip(inputs, local))
+    ]
+    for load in loads:
+        load.start()
+    coords_ref, types_ref, slot_ref, pairs_ref, excl_ref, sigma_ref, well_ref, charge_ref = local
     row, col = lax.axis_index("row"), lax.axis_index("col")
     barrier = greet_peers(n_row, n_col)
+    for load in loads:
+        load.wait()
     slot = slot_ref[...]
     own = []
     lane, chunk = slot & (LANES - 1), slot >> 7
@@ -58,7 +68,7 @@
         all_ref[mine, comp * BLOCKS : (comp + 1) * BLOCKS, :] = total
         own.append(total)
     pairs = pairs_ref[...].astype(jnp.float32)
-    count = jnp.broadcast_to(count_ref[...].astype(jnp.float32), (1, LANES))
+    count = jnp.full((1, LANES), count_ref[0], jnp.int32).astype(jnp.float32)
     all_ref[mine, 32:40, :] = jnp.concatenate(
         [pairs, count, jnp.zeros((5, LANES), jnp.float32)], axis=0
     )
@@ -109,6 +119,7 @@
     for there in sends + passes:
         there.wait_send()
     meta_ref[...] = all_ref[:, 32:40, :].astype(jnp.int32)
+    meta_ref[0, 3:4, :] = jnp.full((1, LANES), mine, jnp.int32)
 
 
 def split(value):
@@ -271,10 +282,10 @@
 
 
 def force_kernel(
-    n_row, n_col, place_ref, meta_ref, all_ref, sigma_ref, well_ref, charge_ref,
+    n_row, n_col, meta_ref, all_ref, sigma_ref, well_ref, charge_ref,
     own_ref, force_ref, sums_ref, first_list, second_list,
 ):
-    mine = place_ref[0]
+    mine = meta_ref[0, 3, 0]
     n_dev = n_row * n_col
 
     table = type_rows(sigma_ref, well_ref, charge_ref)
@@ -419,6 +430,9 @@
     smem = pl.BlockSpec(memory_space=pltpu.SMEM)
     dma = pltpu.SemaphoreType.DMA
     tables = [t.reshape(1, LANES) for t in (sigma_type, well_type, charge_type)]
+    arrays = [
+        coords, atom_types.reshape(BLOCKS, LANES), slots, block_pairs, exclusion, *tables
+    ]
     gathered, meta, own, inverse = pl.pallas_call(
         functools.partial(exchange_kernel, n_row, n_col),
         out_shape=(
@@ -427,33 +441,31 @@
             jax.ShapeDtypeStruct((BLOCKS * 16, LANES), jnp.float32),
             jax.ShapeDtypeStruct((BLOCKS, LANES), jnp.int32),
         ),
-        in_specs=[vmem] * 9,
+        in_specs=[smem] + [pl.BlockSpec(memory_space=pltpu.HBM)] * 8,
         out_specs=(vmem,) * 4,
-        scratch_shapes=[
-            dma((n_row,)), dma((n_row,)), dma((n_row, n_col)), dma((n_row, n_col)),
+        scratch_shapes=[pltpu.VMEM(a.shape, a.dtype) for a in arrays] + [
+            dma((8,)), dma((n_row,)), dma((n_row,)), dma((n_row, n_col)), dma((n_row, n_col)),
         ],
         compiler_params=pltpu.CompilerParams(
-            collective_id=0, has_side_effects=True, vmem_limit_bytes=32 << 20
+            collective_id=0, has_side_effects=True, vmem_limit_bytes=63 << 20
         ),
         name="exchange",
-    )(coords, atom_types.reshape(BLOCKS, LANES), slots, block_pairs, pair_count.reshape(1, 1),
-      exclusion, *tables)
-    place = (lax.axis_index("row") * n_col + lax.axis_index("col")).reshape(1)
+    )(pair_count, *arrays)
     most = block_pairs.shape[1]
     force = pl.pallas_call(
         functools.partial(force_kernel, n_row, n_col),
         out_shape=jax.ShapeDtypeStruct((n_dev, 24, LANES), jnp.float32),
-        in_specs=[smem, smem] + [vmem] * 5,
+        in_specs=[smem] + [vmem] * 5,
         out_specs=vmem,
         scratch_shapes=[
             pltpu.VMEM((n_dev * 128, LANES), jnp.float32),
             pltpu.SMEM((most + 1 + UNROLL,), jnp.int32),
             pltpu.SMEM((most + 1 + UNROLL,), jnp.int32),
         ],
-        compiler_params=pltpu.CompilerParams(vmem_limit_bytes=48 << 20),
+        compiler_params=pltpu.CompilerParams(vmem_limit_bytes=63 << 20),
         name="pair_forces",
     )(
-        place, meta, gathered.reshape(n_dev * ROWS, LANES), *tables, own,
+        meta, gathered.reshape(n_dev * ROWS, LANES), *tables, own,
     )
     return pl.pallas_call(
         functools.partial(return_kernel, n_row, n_col),

time: 37.6 us -> 38.9 us (1.035)
  Pallas kernels: 34.6 us -> 36.4 us
  local copies, waits for them, and re-layouts: 1.94 us -> 1.54 us
    pallas_call x1, Pallas kernels: 11.3 us -> 12.4 us  [body(): pl.pallas_call(functools.partial(exchange_kernel, n_row, n_col), out_shap...]
    pallas_call x1, Pallas kernels: 14.4 us -> 15.3 us  [body(): pl.pallas_call(functools.partial(force_kernel, n_row, n_col), out_shape=j...]
    unnamed x17 -> x5, local copies, waits for them, and re-layouts: 1.94 us -> 1.54 us
where the time goes in v2:
time: 38.9 us; the launch traced here: 38.6 us
  Pallas kernels  36.4 us (94%)
  local copies, waits for them, and re-layouts  1.54 us (4%)
  between operations  0.68 us (2%)
    pallas_call x1, Pallas kernels, body(): pl.pallas_call(functools.partial(force_kernel, n_row, n_col), out_shape=j...  15.3 us
    pallas_call x1, Pallas kernels, body(): pl.pallas_call(functools.partial(exchange_kernel, n_row, n_col), out_shap...  12.4 us
    pallas_call x1, Pallas kernels, body(): pl.pallas_call(functools.partial(return_kernel, n_row, n_col), out_shape=...  8.64 us
    unnamed x5, local copies, waits for them, and re-layouts  1.54 us

profile of v2, /device:TPU:0, one launch (start us, length us, event | category | flops | bytes accessed | tf_op | source)
XLA Modules:
  0.0 38.6 jit_solution(8916928008113557120)
XLA Ops:
  0.7 12.4 %exchange.1 = (f32[16,40,128]{2,1,0:T(8,128)}, s32[16,8,128]{2,1,0:T(8,128)}, f32[128,128]{1,0:T(8,128)}, s32[8,128]{1,0:T(8,128)}) custom-call(s32[1]{0:T(128)S(6)} %copy.11.count_ref, f32[3,1024]{1,0:T(4,128)} %refs_0_.1, s32[8,128]{1,0:T(8,128)} %bitcast.7, s32[8,128]{1,0:T(8,128)} %bitcast.8, s32[2,128]{1,0:T(2,128)} %refs_3_.1, s32[8,64]{1,0:T(8,128)} %refs_4_.1, ...), custom_call_target="tpu_custom_call" | custom-call | tf_op jit(solution)/shard_map/exchange/pallas_call | solution.py:436
  13.1 0.0 copy-start.1
  13.1 15.3 %pair_forces.1.force_ref = f32[16,24,128]{2,1,0:T(8,128)} custom-call(s32[16,8,128]{2,1,0:T(8,128)} %get-tuple-element.9.meta_ref, f32[640,128]{1,0:T(8,128)} %bitcast.6, f32[1,128]{1,0:T(1,128)} %bitcast.10, f32[1,128]{1,0:T(1,128)} %bitcast.12, f32[1,128]{1,0:T(1,128)} %bitcast.14, f32[128,128]{1,0:T(8,128)} %get-tuple-element.11.own_ref), custom_call_target="tpu_custom_call" | custom-call | tf_op jit(solution)/shard_map/pair_forces/pallas_call | solution.py:455
  28.4 0.0 copy-done.1
  28.4 0.0 copy-start
  28.4 0.9 %copy-done = f32[16,24,128]{2,1,0:T(8,128)S(1)} copy-done((f32[16,24,128]{2,1,0:T(8,128)S(1)}, f32[16,24,128]{2,1,0:T(8,128)}, u32[]{:S(2)}) %copy-start) | copy-done | bytes 196632
  29.4 8.6 %return_forces.1 = f32[3,1024]{1,0:T(4,128)S(1)} custom-call(f32[16,24,128]{2,1,0:T(8,128)S(1)} %copy-done, s32[8,128]{1,0:T(8,128)S(1)} %copy-done.1), custom_call_target="tpu_custom_call" | custom-call | tf_op jit(solution)/shard_map/return_forces/pallas_call | solution.py:470
  38.0 0.6 %copy.12 = f32[3,1024]{1,0:T(4,128)} copy(f32[3,1024]{1,0:T(4,128)S(1)} %return_forces.1) | data formatting | bytes 24576
Async XLA Ops:
  13.1 15.4 %copy-start.1 = (s32[8,128]{1,0:T(8,128)S(1)}, s32[8,128]{1,0:T(8,128)}, u32[]{:S(2)}) copy-start(s32[8,128]{1,0:T(8,128)} %get-tuple-element.12.inv_ref) | copy-start | bytes 12292
  28.4 0.9 %copy-start = (f32[16,24,128]{2,1,0:T(8,128)S(1)}, f32[16,24,128]{2,1,0:T(8,128)}, u32[]{:S(2)}) copy-start(f32[16,24,128]{2,1,0:T(8,128)} %pair_forces.1.force_ref) | copy-start | bytes 589828
